TPU v7x, 128 devices: a whole 4x4x4 slice. The times are simulated.
128 devices in a mesh: ctx: 16 (over z_hi, y, core), hd: 8 (over z_lo, x).
Axes of the slice: x: 4, y: 4, z: 4 (z_hi: 2, z_lo: 2; z = z_hi * 2 + z_lo), core: 2. Of those that a mesh axis runs over, the one named last changes fastest.
Arguments:
- block_input: bfloat16 [16384, 1024], P(('hd', 'ctx')), may hold values from -6 to 6
- out_grad: bfloat16 [16384, 1024], P(('hd', 'ctx')), may hold values from -6 to 6
- doc_ids: int32 [16384], replicated, may hold values from 0 to 3, as said below
- w_query: bfloat16 [1024, 1024], P('ctx', 'hd'), may hold values from -0.1875 to 0.1875
- w_key: bfloat16 [1024, 512], P('ctx', 'hd'), may hold values from -0.1875 to 0.1875
- w_value: bfloat16 [1024, 512], P('ctx', 'hd'), may hold values from -0.1875 to 0.1875
- w_out: bfloat16 [1024, 1024], P('ctx', 'hd'), may hold values from -0.75 to 0.75
- w_gate: bfloat16 [1024, 4608], P('ctx', 'hd'), may hold values from -0.1875 to 0.1875
- w_up: bfloat16 [1024, 4608], P('ctx', 'hd'), may hold values from -0.1875 to 0.1875
- w_down: bfloat16 [4608, 1024], P('hd', 'ctx'), may hold values from -0.09375 to 0.09375
- norm_gains: bfloat16 [2048], P(('ctx', 'hd')), may hold values from 0.5 to 1.5
- head_gains: bfloat16 [128], P(('ctx', 'hd')), may hold values from 0.099609375 to 1.8984375
Outputs:
- block_output: bfloat16 [16384, 1024], P(('hd', 'ctx'))
- input_grad: float32 [16384, 1024], P(('hd', 'ctx'))
- w_query_grad: float32 [1024, 1024], P('ctx', 'hd')
- w_key_grad: float32 [1024, 512], P('ctx', 'hd')
- w_value_grad: float32 [1024, 512], P('ctx', 'hd')
- w_out_grad: float32 [1024, 1024], P('ctx', 'hd')
- w_gate_grad: float32 [1024, 4608], P('ctx', 'hd')
- w_up_grad: float32 [1024, 4608], P('ctx', 'hd')
- w_down_grad: float32 [4608, 1024], P('hd', 'ctx')
- norm_gains_grad: float32 [2048], P(('ctx', 'hd'))
- head_gains_grad: float32 [128], P(('ctx', 'hd'))
Inputs may be any that keep to these rules, and one draw needn't show every extreme that they name: `doc_ids`: document numbers never fall along the tokens; tokens s * 8192 to (s + 1) * 8192 - 1 hold exactly documents 2 s and 2 s + 1, each of 2048 tokens or more.
All inputs are finite; a program needn't handle non-finite values.
Results may differ from a plain program's by a relative error of at most 0.025.
Values may be sent and summed in bfloat16 or wider, within the bound.
No kernel may reach another device: no remote copies, remote signals or barrier semaphores. Data moves between devices by JAX's collectives and lax.ppermute only.
A program may use at most 192 MiB of HBM per device.

v0:
```python
import jax
import jax.numpy as jnp
from jax import lax
from jax.sharding import PartitionSpec as P

D = 1024
H = 16
KVH = 8
DH = 64


epsilon = 1e-06
theta = 1000000.0
big_negative = -1e30


def norm_rows(values, scales):
    return values * lax.rsqrt(jnp.mean(values * values, axis=-1, keepdims=True) + epsilon) * scales


def rotary_tables(positions, head_size):
    halfway = head_size // 2
    frequency = theta ** (-(jnp.arange(halfway, dtype=jnp.float32) * 2.0 / head_size))
    angles = positions.astype(jnp.float32)[:, None] * frequency[None, :]
    return (jnp.cos(angles), jnp.sin(angles))


def head_rope(raw_value, scales, cosine, sine_table, head_count):
    row_count = raw_value.shape[0]
    head_size = raw_value.shape[1] // head_count
    halfway = head_size // 2
    shaped = norm_rows(raw_value.reshape(row_count, head_count, head_size), scales)
    leading = shaped[..., :halfway]
    trailing = shaped[..., halfway:]
    cos_wide = cosine[:, None, :]
    sin_wide = sine_table[:, None, :]
    turned = jnp.concatenate(
        [leading * cos_wide - trailing * sin_wide, trailing * cos_wide + leading * sin_wide],
        axis=-1,
    )
    return turned.reshape(row_count, head_count * head_size)


def silu_product(gate_value, up_value):
    return jax.nn.silu(gate_value) * up_value


def contract_last(left, right):
    return lax.dot_general(
        left, right, (((1,), (1,)), ((), ())), preferred_element_type=jnp.float32
    )


def contract_first(left, right):
    return lax.dot_general(
        left, right, (((0,), (0,)), ((), ())), preferred_element_type=jnp.float32
    )


def masked_scores(query_part, key_part, query_marks, key_marks, scale):
    raw_scores = (
        jnp.einsum("sqagd,skad->sagqk", query_part, key_part, preferred_element_type=jnp.float32)
        * scale
    )
    allowed = (query_marks[0][:, :, None] == key_marks[0][:, None, :]) & (
        key_marks[1][:, None, :] <= query_marks[1][:, :, None]
    )
    return (jnp.where(allowed[:, None, None], raw_scores, big_negative), allowed)


def block_stats(running, query_part, key_part, query_marks, key_marks, scale):
    scores, allowed = masked_scores(query_part, key_part, query_marks, key_marks, scale)
    top_new = jnp.maximum(running[0], jnp.max(scores, axis=-1))
    weights = jnp.where(allowed[:, None, None], jnp.exp(scores - top_new[..., None]), 0.0)
    total_new = running[1] * jnp.exp(running[0] - top_new) + jnp.sum(weights, axis=-1)
    return (top_new, total_new)


def block_output(
    running, query_part, key_part, value_part, log_total, query_marks, key_marks, scale
):
    scores = masked_scores(query_part, key_part, query_marks, key_marks, scale)[0]
    weights = jnp.exp(scores - log_total[..., None]).astype(jnp.bfloat16)
    return running + jnp.einsum(
        "sagqk,skad->sqagd", weights, value_part, preferred_element_type=jnp.float32
    )


def block_grads(
    query_part, key_part, value_part, grad_out, log_total, delta_rows, query_marks, key_marks, scale
):
    scores = masked_scores(query_part, key_part, query_marks, key_marks, scale)[0]
    probs = jnp.exp(scores - log_total[..., None])
    grad_value = jnp.einsum(
        "sagqk,sqagd->skad",
        probs.astype(jnp.bfloat16),
        grad_out,
        preferred_element_type=jnp.float32,
    )
    grad_probs = jnp.einsum(
        "sqagd,skad->sagqk", grad_out, value_part, preferred_element_type=jnp.float32
    )
    grad_scores = (probs * (grad_probs - delta_rows[..., None])).astype(jnp.bfloat16)
    grad_query = (
        jnp.einsum("sagqk,skad->sqagd", grad_scores, key_part, preferred_element_type=jnp.float32)
        * scale
    )
    grad_key = (
        jnp.einsum("sagqk,sqagd->skad", grad_scores, query_part, preferred_element_type=jnp.float32)
        * scale
    )
    return (grad_query, grad_key, grad_value)


def shards(
    block_input,
    out_grad,
    doc_ids,
    w_query,
    w_key,
    w_value,
    w_out,
    w_gate,
    w_up,
    w_down,
    norm_gains,
    head_gains,
):
    tokens_dev = block_input.shape[0]
    ctx_count = lax.axis_size("ctx")
    hd_count = lax.axis_size("hd")
    ctx_index = lax.axis_index("ctx")
    hd_index = lax.axis_index("hd")
    seq_count = max(1, hd_count // 4)
    seq_length = tokens_dev * ctx_count * hd_count // seq_count
    head_local = H // hd_count
    kv_local = KVH // hd_count
    share = H // KVH
    head_rows = hd_count * tokens_dev
    group_rows = head_rows // seq_count
    half_rows = group_rows // 2
    scale = DH ** (-0.5)
    weight_query, weight_key, weight_value, weight_out, gains_norm, gains_head = (
        lax.all_gather(w_query, "hd", axis=1, tiled=True),
        lax.all_gather(w_key, "hd", axis=1, tiled=True),
        lax.all_gather(w_value, "hd", axis=1, tiled=True),
        lax.all_gather(w_out, "hd", axis=1, tiled=True),
        lax.all_gather(norm_gains, "hd", axis=0, tiled=True),
        lax.all_gather(head_gains, "hd", axis=0, tiled=True),
    )
    (
        weight_query,
        weight_key,
        weight_value,
        weight_out,
        weight_gate,
        weight_up,
        weight_down,
        gains_norm,
        gains_head,
    ) = (
        lax.all_gather(weight_query, "ctx", axis=0, tiled=True),
        lax.all_gather(weight_key, "ctx", axis=0, tiled=True),
        lax.all_gather(weight_value, "ctx", axis=0, tiled=True),
        lax.all_gather(weight_out, "ctx", axis=0, tiled=True),
        lax.all_gather(w_gate, "ctx", axis=0, tiled=True),
        lax.all_gather(w_up, "ctx", axis=0, tiled=True),
        lax.all_gather(w_down, "ctx", axis=1, tiled=True),
        lax.all_gather(gains_norm, "ctx", axis=0, tiled=True),
        lax.all_gather(gains_head, "ctx", axis=0, tiled=True),
    )
    weight_gate, weight_up, weight_down = (
        lax.all_gather(weight_gate, "hd", axis=1, tiled=True),
        lax.all_gather(weight_up, "hd", axis=1, tiled=True),
        lax.all_gather(weight_down, "hd", axis=0, tiled=True),
    )
    gains_norm = gains_norm.astype(jnp.float32)
    gains_head = gains_head.astype(jnp.float32)
    gain_first = gains_norm[:D]
    gain_second = gains_norm[D:]
    head_first = gains_head[:DH]
    head_second = gains_head[DH:]
    input_f32 = block_input.astype(jnp.float32)
    token_steps = jnp.arange(tokens_dev, dtype=jnp.int32)
    own_index = (hd_index * ctx_count + ctx_index) * tokens_dev + token_steps
    cosine, sine_table = rotary_tables(own_index % seq_length, DH)
    normed = norm_rows(input_f32, gain_first).astype(jnp.bfloat16)
    query_raw = jnp.dot(normed, weight_query, preferred_element_type=jnp.float32)
    key_raw = jnp.dot(normed, weight_key, preferred_element_type=jnp.float32)
    value_low = jnp.dot(normed, weight_value, preferred_element_type=jnp.float32).astype(
        jnp.bfloat16
    )
    query_low = head_rope(query_raw, head_first, cosine, sine_table, H).astype(jnp.bfloat16)
    key_low = head_rope(key_raw, head_second, cosine, sine_table, KVH).astype(jnp.bfloat16)
    kv_tokens = jnp.concatenate(
        [key_low.reshape(tokens_dev, KVH, DH), value_low.reshape(tokens_dev, KVH, DH)], axis=-1
    ).reshape(tokens_dev, KVH * 2 * DH)
    query_heads, kv_heads = (
        lax.all_to_all(query_low, "hd", split_axis=1, concat_axis=0, tiled=True),
        lax.all_to_all(kv_tokens, "hd", split_axis=1, concat_axis=0, tiled=True),
    )
    kv_every = lax.all_gather(kv_heads, "ctx", axis=0, tiled=True)
    span_order = jnp.arange(hd_count, dtype=jnp.int32)
    ids_grid = doc_ids.reshape(hd_count, ctx_count, tokens_dev)

    def block_marks(source):
        index_rows = (
            (span_order[:, None] * ctx_count + source) * tokens_dev + token_steps[None, :]
        ).reshape(seq_count, group_rows)
        id_rows = lax.dynamic_index_in_dim(ids_grid, source, axis=1, keepdims=False).reshape(
            seq_count, group_rows
        )
        return (id_rows, index_rows)

    def key_parts(source):
        block = lax.dynamic_slice_in_dim(kv_every, source * head_rows, head_rows, 0).reshape(
            seq_count, group_rows, kv_local, 2 * DH
        )
        return (block[..., :DH], block[..., DH:], block_marks(source))

    def lower_marks(marks):
        return (marks[0][:, :half_rows], marks[1][:, :half_rows])

    query_marks = block_marks(ctx_index)
    query_grid = query_heads.reshape(seq_count, group_rows, kv_local, share, DH)
    query_lower = query_grid[:, :half_rows]
    query_upper = query_grid[:, half_rows:]
    marks_lower = lower_marks(query_marks)
    marks_upper = (query_marks[0][:, half_rows:], query_marks[1][:, half_rows:])
    sources = jnp.arange(ctx_count, dtype=jnp.int32)
    stat_shape = (seq_count, kv_local, share, half_rows)
    stat_start = (
        jnp.full(stat_shape, big_negative, jnp.float32),
        jnp.zeros(stat_shape, jnp.float32),
    )

    def stats_step(running, source):
        keys_now, values_now, key_marks = key_parts(source)
        lower = block_stats(
            running[0],
            query_lower,
            keys_now[:, :half_rows],
            marks_lower,
            lower_marks(key_marks),
            scale,
        )
        upper = block_stats(running[1], query_upper, keys_now, marks_upper, key_marks, scale)
        return ((lower, upper), None)

    stat_pair, ignored = lax.scan(stats_step, (stat_start, stat_start), sources)
    lse_lower = stat_pair[0][0] + jnp.log(stat_pair[0][1])
    lse_upper = stat_pair[1][0] + jnp.log(stat_pair[1][1])
    out_start = jnp.zeros((seq_count, half_rows, kv_local, share, DH), jnp.float32)

    def output_step(running, source):
        keys_now, values_now, key_marks = key_parts(source)
        lower = block_output(
            running[0],
            query_lower,
            keys_now[:, :half_rows],
            values_now[:, :half_rows],
            lse_lower,
            marks_lower,
            lower_marks(key_marks),
            scale,
        )
        upper = block_output(
            running[1], query_upper, keys_now, values_now, lse_upper, marks_upper, key_marks, scale
        )
        return ((lower, upper), None)

    out_pair, ignored = lax.scan(output_step, (out_start, out_start), sources)
    outputs = jnp.concatenate([out_pair[0], out_pair[1]], axis=1)
    out_low = outputs.reshape(head_rows, head_local * DH).astype(jnp.bfloat16)
    mixed_tokens = lax.all_to_all(out_low, "hd", split_axis=0, concat_axis=1, tiled=True)
    attended = jnp.dot(mixed_tokens, weight_out, preferred_element_type=jnp.float32)
    residual = input_f32 + attended
    normed_second = norm_rows(residual, gain_second).astype(jnp.bfloat16)
    gate_value = jnp.dot(normed_second, weight_gate, preferred_element_type=jnp.float32)
    up_value = jnp.dot(normed_second, weight_up, preferred_element_type=jnp.float32)
    hidden = silu_product(gate_value, up_value).astype(jnp.bfloat16)
    ffn_result = jnp.dot(hidden, weight_down, preferred_element_type=jnp.float32)
    block_output_value = (residual + ffn_result).astype(jnp.bfloat16)
    grad_hidden = contract_last(out_grad, weight_down)
    silu_grads = jax.vjp(silu_product, gate_value, up_value)[1](grad_hidden)
    grad_gate = silu_grads[0].astype(jnp.bfloat16)
    grad_up = silu_grads[1].astype(jnp.bfloat16)
    grad_wdown = contract_first(hidden, out_grad)
    grad_wgate = contract_first(normed_second, grad_gate)
    grad_wup = contract_first(normed_second, grad_up)
    grad_second = contract_last(grad_gate, weight_gate) + contract_last(grad_up, weight_up)
    grad_resid_part, grad_gain_second = jax.vjp(norm_rows, residual, gain_second)[1](grad_second)
    grad_residual = out_grad.astype(jnp.float32) + grad_resid_part
    grad_attended = grad_residual.astype(jnp.bfloat16)
    grad_wout = contract_first(mixed_tokens, grad_attended)
    grad_mixed = contract_last(grad_attended, weight_out).astype(jnp.bfloat16)
    grad_heads = lax.all_to_all(grad_mixed, "hd", split_axis=1, concat_axis=0, tiled=True)
    grad_grid = grad_heads.reshape(seq_count, group_rows, kv_local, share, DH)
    delta_all = jnp.transpose(
        jnp.sum(grad_grid.astype(jnp.float32) * outputs, axis=-1), (0, 2, 3, 1)
    )
    grad_lower = grad_grid[:, :half_rows]
    grad_upper = grad_grid[:, half_rows:]
    delta_lower = delta_all[..., :half_rows]
    delta_upper = delta_all[..., half_rows:]

    def grad_step(running, source):
        keys_now, values_now, key_marks = key_parts(source)
        query_low_part, key_low_part, value_low_part = block_grads(
            query_lower,
            keys_now[:, :half_rows],
            values_now[:, :half_rows],
            grad_lower,
            lse_lower,
            delta_lower,
            marks_lower,
            lower_marks(key_marks),
            scale,
        )
        query_high_part, key_high_part, value_high_part = block_grads(
            query_upper,
            keys_now,
            values_now,
            grad_upper,
            lse_upper,
            delta_upper,
            marks_upper,
            key_marks,
            scale,
        )
        padding = ((0, 0), (0, group_rows - half_rows), (0, 0), (0, 0))
        grad_keys = key_high_part + jnp.pad(key_low_part, padding)
        grad_values = value_high_part + jnp.pad(value_low_part, padding)
        packed_block = jnp.concatenate([grad_keys, grad_values], axis=-1).reshape(
            head_rows, kv_local * 2 * DH
        )
        return ((running[0] + query_low_part, running[1] + query_high_part), packed_block)

    query_pair, kv_blocks = lax.scan(grad_step, (out_start, out_start), sources)
    kv_grad_terms = kv_blocks.reshape(ctx_count * head_rows, kv_local * 2 * DH)
    kv_grad_mine = lax.psum_scatter(kv_grad_terms, "ctx", scatter_dimension=0, tiled=True)
    grad_query_heads = (
        jnp.concatenate([query_pair[0], query_pair[1]], axis=1)
        .reshape(head_rows, head_local * DH)
        .astype(jnp.bfloat16)
    )
    grad_query_tok, grad_kv_tok = (
        lax.all_to_all(grad_query_heads, "hd", split_axis=0, concat_axis=1, tiled=True),
        lax.all_to_all(
            kv_grad_mine.astype(jnp.bfloat16), "hd", split_axis=0, concat_axis=1, tiled=True
        ),
    )
    grad_kv = grad_kv_tok.reshape(tokens_dev, KVH, 2 * DH)
    grad_key_turned = grad_kv[..., :DH].reshape(tokens_dev, KVH * DH)
    grad_value = grad_kv[..., DH:].reshape(tokens_dev, KVH * DH)

    def query_rope(raw_value, scales):
        return head_rope(raw_value, scales, cosine, sine_table, H)

    def key_rope(raw_value, scales):
        return head_rope(raw_value, scales, cosine, sine_table, KVH)

    grad_query_raw, grad_head_first = jax.vjp(query_rope, query_raw, head_first)[1](
        grad_query_tok.astype(jnp.float32)
    )
    grad_key_raw, grad_head_second = jax.vjp(key_rope, key_raw, head_second)[1](
        grad_key_turned.astype(jnp.float32)
    )
    grad_query_raw = grad_query_raw.astype(jnp.bfloat16)
    grad_key_raw = grad_key_raw.astype(jnp.bfloat16)
    grad_wquery = contract_first(normed, grad_query_raw)
    grad_wkey = contract_first(normed, grad_key_raw)
    grad_wvalue = contract_first(normed, grad_value)
    grad_normed = (
        contract_last(grad_query_raw, weight_query)
        + contract_last(grad_key_raw, weight_key)
        + contract_last(grad_value, weight_value)
    )
    grad_input_part, grad_gain_first = jax.vjp(norm_rows, input_f32, gain_first)[1](grad_normed)
    input_grad = grad_residual + grad_input_part
    gain_grads = jnp.concatenate([grad_gain_first, grad_gain_second])
    head_grads = jnp.concatenate([grad_head_first, grad_head_second])
    grad_wgate, grad_wup, grad_wdown = (
        lax.psum_scatter(grad_wgate, "hd", scatter_dimension=1, tiled=True),
        lax.psum_scatter(grad_wup, "hd", scatter_dimension=1, tiled=True),
        lax.psum_scatter(grad_wdown, "hd", scatter_dimension=0, tiled=True),
    )
    (
        grad_wquery,
        grad_wkey,
        grad_wvalue,
        grad_wout,
        grad_wgate,
        grad_wup,
        grad_wdown,
        gain_grads,
        head_grads,
    ) = (
        lax.psum_scatter(grad_wquery, "ctx", scatter_dimension=0, tiled=True),
        lax.psum_scatter(grad_wkey, "ctx", scatter_dimension=0, tiled=True),
        lax.psum_scatter(grad_wvalue, "ctx", scatter_dimension=0, tiled=True),
        lax.psum_scatter(grad_wout, "ctx", scatter_dimension=0, tiled=True),
        lax.psum_scatter(grad_wgate, "ctx", scatter_dimension=0, tiled=True),
        lax.psum_scatter(grad_wup, "ctx", scatter_dimension=0, tiled=True),
        lax.psum_scatter(grad_wdown, "ctx", scatter_dimension=1, tiled=True),
        lax.psum_scatter(gain_grads, "ctx", scatter_dimension=0, tiled=True),
        lax.psum_scatter(head_grads, "ctx", scatter_dimension=0, tiled=True),
    )
    grad_wquery, grad_wkey, grad_wvalue, grad_wout, gain_grads, head_grads = (
        lax.psum_scatter(grad_wquery, "hd", scatter_dimension=1, tiled=True),
        lax.psum_scatter(grad_wkey, "hd", scatter_dimension=1, tiled=True),
        lax.psum_scatter(grad_wvalue, "hd", scatter_dimension=1, tiled=True),
        lax.psum_scatter(grad_wout, "hd", scatter_dimension=1, tiled=True),
        lax.psum_scatter(gain_grads, "hd", scatter_dimension=0, tiled=True),
        lax.psum_scatter(head_grads, "hd", scatter_dimension=0, tiled=True),
    )
    return (
        block_output_value,
        input_grad,
        grad_wquery,
        grad_wkey,
        grad_wvalue,
        grad_wout,
        grad_wgate,
        grad_wup,
        grad_wdown,
        gain_grads,
        head_grads,
    )


def solution(mesh):
    return jax.shard_map(
        shards,
        mesh=mesh,
        in_specs=(
            P(("hd", "ctx"), None),
            P(("hd", "ctx"), None),
            P(),
            P("ctx", "hd"),
            P("ctx", "hd"),
            P("ctx", "hd"),
            P("ctx", "hd"),
            P("ctx", "hd"),
            P("ctx", "hd"),
            P("hd", "ctx"),
            P(("ctx", "hd")),
            P(("ctx", "hd")),
        ),
        out_specs=(
            P(("hd", "ctx"), None),
            P(("hd", "ctx"), None),
            P("ctx", "hd"),
            P("ctx", "hd"),
            P("ctx", "hd"),
            P("ctx", "hd"),
            P("ctx", "hd"),
            P("ctx", "hd"),
            P("hd", "ctx"),
            P(("ctx", "hd")),
            P(("ctx", "hd")),
        ),
        check_vma=False,
    )
```

profile of v0, /device:TPU:0, one launch (start us, length us, event | category | flops | bytes accessed | tf_op | source)
XLA Modules:
  0.0 2430.8 jit_solution(11490778222827153728)
XLA Ops:
  8.1 29.1 %all_gather.63 = bf16[64,512]{0,1:T(8,128)(2,1)S(1)} all-gather(bf16[64,64]{0,1:T(8,128)(2,1)S(1)} %copy.199), channel_id=1, replica_groups=mesh['ctx'=16,'hd'=8] {'hd'}, dimensions={1}, use_global_device_ids=true | all-gather | bytes 73728 | tf_op jit(solution)/shard_map/all_gather | solution.py:146
  38.7 28.2 %all_gather.59 = bf16[64,512]{0,1:T(8,128)(2,1)S(1)} all-gather(bf16[64,64]{0,1:T(8,128)(2,1)S(1)} %copy.196), channel_id=1, replica_groups=mesh['ctx'=16,'hd'=8] {'hd'}, dimensions={1}, use_global_device_ids=true | all-gather | bytes 73728 | tf_op jit(solution)/shard_map/all_gather | solution.py:145
  69.1 25.7 %all_gather.66 = bf16[64,1024]{1,0:T(8,128)(2,1)} all-gather(bf16[64,128]{1,0:T(8,128)(2,1)} %param.21), channel_id=1, replica_groups=mesh['ctx'=16,'hd'=8] {'hd'}, dimensions={1}, use_global_device_ids=true | all-gather | bytes 147456 | tf_op jit(solution)/shard_map/all_gather | solution.py:144
  99.8 17.8 all-reduce.15
  117.6 25.0 %all-gather = bf16[16,1,128]{2,1,0:T(2,128)(2,1)S(1)} all-gather(bf16[1,1,128]{2,1,0:T(2,128)(2,1)S(1)} %bitcast.661), channel_id=1, replica_groups=mesh['ctx'=16,'hd'=8] {'ctx'}, dimensions={0}, use_global_device_ids=true | all-gather | bytes 4352 | tf_op jit(solution)/shard_map/all_gather | solution.py:169
  144.6 33.6 %all-reduce.8 = bf16[128]{0:T(256)(128)(2,1)S(1)} all-reduce(bf16[128]{0:T(256)(128)(2,1)S(1)} %dynamic-update-slice.2), channel_id=1, replica_groups=mesh['ctx'=16,'hd'=8] {'ctx'}, use_global_device_ids=true, to_apply=%add.8 | all-reduce | flops 128 | bytes 512
  193.8 25.0 %all_gather.68 = bf16[64,1024]{1,0:T(8,128)(2,1)} all-gather(bf16[64,128]{1,0:T(8,128)(2,1)S(1)} %copy-done.48), channel_id=1, replica_groups=mesh['ctx'=16,'hd'=8] {'hd'}, dimensions={1}, use_global_device_ids=true | all-gather | bytes 147456 | tf_op jit(solution)/shard_map/all_gather | solution.py:147
  227.9 46.9 %all-gather.19.cloned.1.call-done = bf16[1024,1024]{1,0:T(8,128)(2,1)} async-done(((bf16[64,1024]{1,0:T(8,128)(2,1)}), bf16[1024,1024]{1,0:T(8,128)(2,1)}) %all-gather.19.cloned.1.call-update) | async-done | bytes 2097168 | tf_op jit(solution)/shard_map/all_gather | solution.py:162
  284.8 37.0 %all-gather.31.cloned.1.call-done = bf16[576,1024]{0,1:T(8,128)(2,1)} async-done(((bf16[576,64]{0,1:T(8,128)(2,1)}), bf16[576,1024]{0,1:T(8,128)(2,1)}) %all-gather.31.cloned.1.call-update) | async-done | bytes 1179664 | tf_op jit(solution)/shard_map/all_gather | solution.py:168
  324.8 54.7 %all-gather.17.cloned.1.call-done = bf16[16384,128]{1,0:T(8,128)(2,1)} async-done(((bf16[1024,128]{1,0:T(8,128)(2,1)}), bf16[16384,128]{1,0:T(8,128)(2,1)}) %all-gather.17.cloned.1.call-update) | async-done | bytes 4194320 | tf_op jit(solution)/shard_map/all_gather | solution.py:202
  379.6 126.0 %while.47 = (s32[]{:T(128)}, f32[2,1,2,256]{3,2,0,1:T(2,128)S(1)}, f32[2,1,2,256]{3,2,0,1:T(2,128)S(1)}, f32[2,1,2,256]{3,2,0,1:T(2,128)S(1)}, f32[2,1,2,256]{3,...) while((s32[]{:T(128)}, f32[2,1,2,256]{3,2,0,1:T(2,128)S(1)}, ...), condition=%wide.region_8.9_spmd.clone, body=%wide.region_3.8_spmd.clone.sunk | while | flops 107621408 | bytes 8819105 | solution.py:250
  506.8 144.4 %while.48 = (s32[]{:T(128)}, f32[2,256,1,2,64]{1,4,3,0,2:T(8,128)S(1)}, f32[2,256,1,2,64]{1,4,3,0,2:T(8,128)S(1)}, s32[16]{0:T(128)S(1)}, bf16[16384,128]{1,0:T(...) while((s32[]{:T(128)}, ...), condition=%wide.region_10.11_spmd.clone, body=%wide.region_9.10_spmd.clone.sunk | while | flops 205915168 | bytes 3477920 | solution.py:272
  686.3 51.9 %all-gather.33.cloned.1.call-done = bf16[4608,1024]{1,0:T(8,128)(2,1)} async-done(((bf16[576,1024]{1,0:T(8,128)(2,1)}), bf16[4608,1024]{1,0:T(8,128)(2,1)}) %all-gather.33.cloned.1.call-update) | async-done | bytes 9437200 | tf_op jit(solution)/shard_map/all_gather | solution.py:175
  738.2 10.1 multiply_convert_fusion
  772.8 263.7 %while.49 = (s32[]{:T(128)}, f32[2,256,1,2,64]{1,4,3,0,2:T(8,128)}, f32[2,256,1,2,64]{1,4,3,0,2:T(8,128)}, f32[16,1024,128]{2,1,0:T(8,128)}, s32[16]{0:T(128)}, ...) while((s32[]{:T(128)}, f32[2,256,1,2,64]{1,4,3,0,2:T(8,128)}, ...), condition=%wide.region_15.16_spmd.clone, body=%wide.region_14.15_spmd.clone.sunk | while | flops 510755872 | bytes 26162232 | solution.py:339
  1036.6 101.7 %reduce-scatter.26.cloned.1.call-done = f32[1024,128]{1,0:T(8,128)} async-done(((f32[16384,128]{1,0:T(8,128)}), f32[1024,128]{1,0:T(8,128)}) %reduce-scatter.26.cloned.1.call-update) | async-done | bytes 524304 | tf_op jit(solution)/shard_map/reduce_scatter | solution.py:341
  1139.6 11.4 all_to_all.88
  1159.7 9.8 all_to_all.89
  1200.5 21.4 reduce-scatter.32.cloned.1.call-done
  1223.8 71.9 %reduce-scatter.34.cloned.1.call-done = f32[64,512]{1,0:T(8,128)} async-done(((f32[1024,512]{1,0:T(8,128)}), f32[64,512]{1,0:T(8,128)}) %reduce-scatter.34.cloned.1.call-update) | async-done | bytes 131088 | tf_op jit(solution)/shard_map/reduce_scatter | solution.py:401
  1297.5 81.7 %reduce-scatter.36.cloned.1.call-done = f32[64,1024]{1,0:T(8,128)} async-done(((f32[1024,1024]{1,0:T(8,128)}), f32[64,1024]{1,0:T(8,128)}) %reduce-scatter.36.cloned.1.call-update) | async-done | bytes 262160 | tf_op jit(solution)/shard_map/reduce_scatter | solution.py:402
  1379.2 83.3 %reduce-scatter.28.cloned.1.call-done = f32[64,1024]{1,0:T(8,128)} async-done(((f32[1024,1024]{1,0:T(8,128)}), f32[64,1024]{1,0:T(8,128)}) %reduce-scatter.28.cloned.1.call-update) | async-done | bytes 262160 | tf_op jit(solution)/shard_map/reduce_scatter | solution.py:399
  1462.6 191.8 %reduce-scatter.40.cloned.1.call-done = f32[1024,576]{0,1:T(8,128)} async-done(((f32[1024,4608]{0,1:T(8,128)}), f32[1024,576]{0,1:T(8,128)}) %reduce-scatter.40.cloned.1.call-update) | async-done | bytes 2359312 | tf_op jit(solution)/shard_map/reduce_scatter | solution.py:384
  1657.7 188.9 %reduce-scatter.42.cloned.1.call-done = f32[1024,576]{0,1:T(8,128)} async-done(((f32[1024,4608]{0,1:T(8,128)}), f32[1024,576]{0,1:T(8,128)}) %reduce-scatter.42.cloned.1.call-update) | async-done | bytes 2359312 | tf_op jit(solution)/shard_map/reduce_scatter | solution.py:385
  1849.9 189.1 %reduce-scatter.44.cloned.1.call-done = f32[576,1024]{1,0:T(8,128)} async-done(((f32[4608,1024]{1,0:T(8,128)}), f32[576,1024]{1,0:T(8,128)}) %reduce-scatter.44.cloned.1.call-update) | async-done | bytes 2359312 | tf_op jit(solution)/shard_map/reduce_scatter | solution.py:386
  2052.6 38.7 %all-reduce.13 = (f32[2048]{0:T(1024)S(1)}, f32[128]{0:T(128)S(1)}) all-reduce(f32[2048]{0:T(1024)S(1)} %pad_maximum_fusion.4, f32[128]{0:T(128)S(1)} %pad_maximum_fusion.5), channel_id=17, replica_groups=mesh['ctx'=16,'hd'=8] {'ctx'}, use_global_device_ids=true, to_apply=%region_36.37.clone | all-reduce | flops 2176 | bytes 17408
  2091.5 16.4 all-reduce.14
  2117.1 37.5 %reduce-scatter.38.cloned.1.call-done = f32[64,128]{1,0:T(8,128)} async-done(((f32[64,1024]{1,0:T(8,128)}), f32[64,128]{1,0:T(8,128)}) %reduce-scatter.38.cloned.1.call-update) | async-done | bytes 32784 | tf_op jit(solution)/shard_map/reduce_scatter | solution.py:413
  2154.6 39.1 %reduce-scatter.30.cloned.1.call-done = f32[64,128]{1,0:T(8,128)} async-done(((f32[64,1024]{1,0:T(8,128)}), f32[64,128]{1,0:T(8,128)}) %reduce-scatter.30.cloned.1.call-update) | async-done | bytes 32784 | tf_op jit(solution)/shard_map/reduce_scatter | solution.py:410
  2193.8 76.4 %reduce-scatter.50.cloned.1.call-done = f32[64,576]{1,0:T(8,128)} async-done(((f32[1024,576]{1,0:T(8,128)}), f32[64,576]{1,0:T(8,128)}) %reduce-scatter.50.cloned.1.call-update) | async-done | bytes 147472
  2270.2 77.2 %reduce-scatter.52.cloned.1.call-done = f32[64,576]{1,0:T(8,128)} async-done(((f32[1024,576]{1,0:T(8,128)}), f32[64,576]{1,0:T(8,128)}) %reduce-scatter.52.cloned.1.call-update) | async-done | bytes 147472
  2347.4 76.6 %reduce-scatter.54.cloned.1.call-done = f32[64,576]{1,0:T(8,128)} async-done(((f32[1024,576]{1,0:T(8,128)}), f32[64,576]{1,0:T(8,128)}) %reduce-scatter.54.cloned.1.call-update) | async-done | bytes 147472
  (1443 shorter events, 588.7 us)
Async XLA Ops:
  7.2 173.1 %copy-start = (bf16[128,1024]{1,0:T(8,128)(2,1)S(1)}, bf16[128,1024]{1,0:T(8,128)(2,1)}, u32[]{:S(2)}) copy-start(bf16[128,1024]{1,0:T(8,128)(2,1)} %param.18) | copy-start | bytes 786436
  7.2 171.3 %all-gather.15.cloned.1.call-start = ((), (), s32[]{:S(2)}) async-start(), calls=%async_computation.22 | async-start | bytes 1114112 | tf_op jit(solution)/shard_map/all_gather | solution.py:164
  37.9 142.4 %all-gather.13.cloned.1.call-start = ((), (), s32[]{:S(2)}) async-start(), calls=%async_computation.21 | async-start | bytes 1114112 | tf_op jit(solution)/shard_map/all_gather | solution.py:163
  67.7 151.2 %all-gather.23.cloned.1.call-start = ((), (), s32[]{:S(2)}) async-start(), calls=%async_computation.26 | async-start | bytes 1392640 | tf_op jit(solution)/shard_map/all_gather | solution.py:166
  68.5 157.0 %all-gather.27.cloned.1.call-start = ((), (), s32[]{:S(2)}) async-start(), calls=%async_computation.28 | async-start | bytes 1392640 | tf_op jit(solution)/shard_map/all_gather | solution.py:167
  69.0 205.8 %all-gather.19.cloned.1.call-start = ((), (), s32[]{:S(2)}) async-start(), calls=%async_computation.24 | async-start | bytes 2228224 | tf_op jit(solution)/shard_map/all_gather | solution.py:162
  94.8 227.0 %all-gather.31.cloned.1.call-start = ((), (), s32[]{:S(2)}) async-start(), calls=%async_computation.30 | async-start | bytes 1392640 | tf_op jit(solution)/shard_map/all_gather | solution.py:168
  95.4 284.2 %all-gather.17.cloned.1.call-start = ((), (), s32[]{:S(2)}) async-start(), calls=%async_computation.23 | async-start | bytes 4456448 | tf_op jit(solution)/shard_map/all_gather | solution.py:202
  193.7 463.7 %all-gather.21.cloned.1.call-start = ((), (), s32[]{:S(2)}) async-start(), calls=%async_computation.25 | async-start | bytes 2228224 | tf_op jit(solution)/shard_map/all_gather | solution.py:165
  218.8 450.5 %all-gather.25.cloned.1.call-start = ((), (), s32[]{:S(2)}) async-start(), calls=%async_computation.27 | async-start | bytes 10616832 | tf_op jit(solution)/shard_map/all_gather | solution.py:173
  221.4 456.5 %all-gather.29.cloned.1.call-start = ((), (), s32[]{:S(2)}) async-start(), calls=%async_computation.29 | async-start | bytes 10616832 | tf_op jit(solution)/shard_map/all_gather | solution.py:174
  279.1 45.1 %all-to-all-start.1 = ((bf16[128,8,128]{0,2,1:T(8,128)(2,1)}), bf16[128,8,128]{0,2,1:T(8,128)(2,1)S(1)}, u32[]{:S(2)}, u32[]{:S(2)}) async-start(bf16[128,8,128]{0,2,1:T(8,128)(2,1)} %bitcast.12), calls=%async_computation.1 | async-start | bytes 524288 | tf_op jit(solution)/shard_map/all_to_all | solution.py:199
  283.5 454.7 %all-gather.33.cloned.1.call-start = ((), (), s32[]{:S(2)}) async-start(), calls=%async_computation.31 | async-start | bytes 10616832 | tf_op jit(solution)/shard_map/all_gather | solution.py:175
  652.8 14.1 all-to-all-start.2
  759.3 10.9 all-to-all-start.3
  762.8 375.6 %reduce-scatter.26.cloned.1.call-start = ((), (), s32[]{:S(2)}) async-start(), calls=%async_computation.32 | async-start | bytes 8912896 | tf_op jit(solution)/shard_map/reduce_scatter | solution.py:341
  1036.5 114.9 %copy-start.35 = (f32[8,1,128]{2,1,0:T(1,128)S(1)}, f32[8,1,128]{2,1,0:T(1,128)}, u32[]{:S(2)}) copy-start(f32[8,1,128]{2,1,0:T(1,128)} %copy-done.34) | copy-start | bytes 12292
  1036.6 114.9 %copy-start.46 = (f32[128]{0:T(128)S(1)}, f32[128]{0:T(128)}, u32[]{:S(2)}) copy-start(f32[128]{0:T(128)} %copy-done.45) | copy-start | bytes 1540
  1036.6 185.4 %reduce-scatter.32.cloned.1.call-start = ((), (), s32[]{:S(2)}) async-start(), calls=%async_computation.35 | async-start | bytes 2228224 | tf_op jit(solution)/shard_map/reduce_scatter | solution.py:400
  1153.4 142.3 %reduce-scatter.34.cloned.1.call-start = ((), (), s32[]{:S(2)}) async-start(), calls=%async_computation.36 | async-start | bytes 2228224 | tf_op jit(solution)/shard_map/reduce_scatter | solution.py:401
  1155.4 223.8 %reduce-scatter.36.cloned.1.call-start = ((), (), s32[]{:S(2)}) async-start(), calls=%async_computation.37 | async-start | bytes 4456448 | tf_op jit(solution)/shard_map/reduce_scatter | solution.py:402
  1158.1 304.4 %reduce-scatter.28.cloned.1.call-start = ((), (), s32[]{:S(2)}) async-start(), calls=%async_computation.33 | async-start | bytes 4456448 | tf_op jit(solution)/shard_map/reduce_scatter | solution.py:399
  1172.8 481.6 %reduce-scatter.40.cloned.1.call-start = ((), (), s32[]{:S(2)}) async-start(), calls=%async_computation.39 | async-start | bytes 21233664 | tf_op jit(solution)/shard_map/reduce_scatter | solution.py:384
  1182.0 664.6 %reduce-scatter.42.cloned.1.call-start = ((), (), s32[]{:S(2)}) async-start(), calls=%async_computation.40 | async-start | bytes 21233664 | tf_op jit(solution)/shard_map/reduce_scatter | solution.py:385
  1191.2 847.7 %reduce-scatter.44.cloned.1.call-start = ((), (), s32[]{:S(2)}) async-start(), calls=%async_computation.41 | async-start | bytes 21233664 | tf_op jit(solution)/shard_map/reduce_scatter | solution.py:386
  1200.5 910.3 %reduce-scatter.46.cloned.1.call-start = ((), (), s32[]{:S(2)}) async-start(), calls=%async_computation.42 | async-start | bytes 294912
  1223.7 891.9 %reduce-scatter.48.cloned.1.call-start = ((), (), s32[]{:S(2)}) async-start(), calls=%async_computation.43 | async-start | bytes 294912
  1297.5 857.2 %reduce-scatter.38.cloned.1.call-start = ((), (), s32[]{:S(2)}) async-start(), calls=%async_computation.38 | async-start | bytes 294912 | tf_op jit(solution)/shard_map/reduce_scatter | solution.py:413
  1379.2 814.6 %reduce-scatter.30.cloned.1.call-start = ((), (), s32[]{:S(2)}) async-start(), calls=%async_computation.34 | async-start | bytes 294912 | tf_op jit(solution)/shard_map/reduce_scatter | solution.py:410
  1462.6 807.6 %reduce-scatter.50.cloned.1.call-start = ((), (), s32[]{:S(2)}) async-start(), calls=%async_computation.44 | async-start | bytes 2785280
  1657.6 689.8 %reduce-scatter.52.cloned.1.call-start = ((), (), s32[]{:S(2)}) async-start(), calls=%async_computation.45 | async-start | bytes 2785280
  1849.8 574.2 %reduce-scatter.54.cloned.1.call-start = ((), (), s32[]{:S(2)}) async-start(), calls=%async_computation.46 | async-start | bytes 2785280
  (115 other events, 1920.8 us)
Sparse Core Ops, SparseCore 0:
  38.0 46.6 all-gather.14
  87.7 43.6 all-gather.12
  133.8 44.5 all-gather.22
  180.7 44.6 all-gather.26
  227.7 47.0 all-gather.18
  277.1 44.6 all-gather.30
  324.8 54.6 all-gather.16
  382.0 47.0 all-gather.20
  430.8 100.4 all-gather.24
  532.7 100.5 all-gather.28
  634.9 103.2 all-gather.32
  1036.6 101.6 reduce-scatter.25
  1153.5 68.4 reduce-scatter.31
  1225.8 69.8 reduce-scatter.33
  1299.6 79.5 reduce-scatter.35
  1383.6 78.8 reduce-scatter.27
  1464.9 189.5 reduce-scatter.39
  1656.7 189.8 reduce-scatter.41
  1849.1 189.8 reduce-scatter.43
  2041.1 35.9 reduce-scatter.45
  2079.7 35.9 reduce-scatter.47
  2118.6 36.0 reduce-scatter.37
  2157.7 36.0 reduce-scatter.29
  2198.2 71.9 reduce-scatter.49
  2275.2 72.1 reduce-scatter.51
  2351.8 72.1 reduce-scatter.53
where the time goes:
time: 2450 us; the launch traced here: 2430 us
  waiting for transfers between devices  1450 us (59%)
  blocking collectives  270 us (11%)
  matrix products  270 us (11%)
  local copies, waits for them, and re-layouts  201 us (8%)
  loops' own time  125 us (5%)
  other arithmetic  77.8 us (3%)
    unnamed x31, waiting for transfers between devices  236 us
    reduce_scatter x1, waiting for transfers between devices, shards(): lax.psum_scatter(grad_wgate, 'hd', scatter_dimension=1, tiled=True)  192 us
    reduce_scatter x1, waiting for transfers between devices, shards(): lax.psum_scatter(grad_wdown, 'hd', scatter_dimension=0, tiled=True)  189 us
    reduce_scatter x1, waiting for transfers between devices, shards(): lax.psum_scatter(grad_wup, 'hd', scatter_dimension=1, tiled=True)  189 us
    unnamed x4, blocking collectives  106 us
    reduce_scatter x1, waiting for transfers between devices, shards(): lax.psum_scatter(kv_grad_terms, 'ctx', scatter_dimension=0, tiled=True)  102 us
    reduce_scatter x1, waiting for transfers between devices, shards(): lax.psum_scatter(grad_wquery, 'ctx', scatter_dimension=0, tiled=True)  83.3 us
    reduce_scatter x1, waiting for transfers between devices, shards(): lax.psum_scatter(grad_wout, 'ctx', scatter_dimension=0, tiled=True)  81.7 us
  transfers between devices with their start and end apart: 29, of which 21 were waited for; matrix products, arithmetic and copies ran while one was open for 12% of the time, Pallas kernels for 0%

commit v1 on v0

v1 whole, which is shorter than its diff:
```python
import jax
import jax.numpy as jnp
from jax import lax
from jax.experimental import pallas as pl
from jax.experimental.pallas import tpu as pltpu
from jax.sharding import Mesh
from jax.sharding import PartitionSpec as P

D = 1024
H = 16
KVH = 8
DH = 64
FF = 4608

epsilon = 1e-06
theta = 1000000.0
bf16 = jnp.bfloat16
f32 = jnp.float32

AXES = ("zh", "y", "c", "zl", "x")
GROUP = ("c", "x")
BLOCKS = ("zh", "y")
SHARDS = ("zh", "y", "zl")

KB = 512


def contract(left, right, dims):
    return lax.dot_general(left, right, ((dims[0], dims[1]), ((), ())), preferred_element_type=f32)


def dot_nn(left, right):
    return contract(left, right, ((1,), (0,)))


def dot_nt(left, right):
    return contract(left, right, ((1,), (1,)))


def dot_tn(left, right):
    return contract(left, right, ((0,), (0,)))


def lanes(shape):
    return lax.broadcasted_iota(jnp.int32, shape, len(shape) - 1)


def swing(values):
    return pltpu.roll(values, 64, 1)


def head_rows(packed, upper):
    low = lanes(packed.shape) < 64
    turned = swing(packed)
    if upper:
        first = jnp.where(low, 0.0, turned)
        second = jnp.where(low, 0.0, packed)
    else:
        first = jnp.where(low, packed, 0.0)
        second = jnp.where(low, turned, 0.0)
    return jnp.concatenate([first, second], axis=0)


def key_block(ref, j):
    return ref[pl.ds(2 * (j % 4), 2), :, j // 4]


def spans(info_ref, x_block):
    start = x_block * 2048 + info_ref[0] * 256
    cut = info_ref[1]
    first_from = jnp.where(start >= cut, cut, 0)
    last_from = jnp.where(start + 255 >= cut, cut, 0)
    low = first_from // KB
    high = start // KB
    middle = jnp.minimum((last_from + KB - 1) // KB, high)
    return start, cut, low, middle, high


def allowed_pairs(start, cut, j, query_dim, shape):
    rows = lax.broadcasted_iota(jnp.int32, shape, query_dim)
    query_at = start + (rows & 255)
    key_at = j * KB + lax.broadcasted_iota(jnp.int32, shape, 1 - query_dim)
    query_from = jnp.where(query_at >= cut, cut, 0)
    return (key_at <= query_at) & (key_at >= query_from)


def with_ones(kv):
    return jnp.where(lanes(kv.shape) < 64, jnp.ones_like(kv), kv)


def attend_kernel(info_ref, q_ref, kv_ref, mixed_ref, low_ref, inverse_ref, acc_ref):
    x_block = pl.program_id(0)
    start, cut, low, middle, high = spans(info_ref, x_block)
    queries = head_rows(q_ref[:, 0].reshape(256, 128).astype(f32), False).astype(bf16)
    acc_ref[...] = jnp.zeros_like(acc_ref)

    def step(masked):
        def body(j, carry):
            kv = key_block(kv_ref, j).reshape(KB, 128)
            weights = jnp.exp(dot_nt(queries, kv))
            if masked:
                allowed = allowed_pairs(start, cut, j, 0, weights.shape)
                weights = jnp.where(allowed, weights, 0.0)
            acc_ref[...] += dot_nn(weights.astype(bf16), with_ones(kv))
            return carry

        return body

    lax.fori_loop(low, middle, step(True), 0)
    lax.fori_loop(middle, high, step(False), 0)
    step(True)(high, 0)
    sums = acc_ref[...]
    turned = swing(sums)
    is_low = lanes((256, 128)) < 64
    first, second = sums[:256], sums[256:]
    first_turned, second_turned = turned[:256], turned[256:]
    inverse = 1.0 / jnp.where(is_low, first, second_turned)
    mixed = jnp.where(is_low, first_turned, second) * inverse
    mixed_ref[...] = mixed.reshape(mixed_ref.shape)
    low_ref[...] = mixed.astype(bf16).reshape(low_ref.shape)
    inverse_ref[...] = inverse.reshape(inverse_ref.shape)


def chunk_spec():
    return pl.BlockSpec((2, 1, 128, 128), lambda i: (0, i, 0, 0))


def whole_spec(shape):
    return pl.BlockSpec(shape, lambda i: (0,) * len(shape))


def attend(info, queries, kv):
    out = jax.ShapeDtypeStruct((2, 4, 128, 128), f32)
    return pl.pallas_call(
        attend_kernel,
        grid=(4,),
        in_specs=[
            pl.BlockSpec(memory_space=pltpu.SMEM),
            chunk_spec(),
            whole_spec((8, 2, 4, 128, 128)),
        ],
        out_specs=[chunk_spec(), chunk_spec(), chunk_spec()],
        out_shape=[out, jax.ShapeDtypeStruct(out.shape, bf16), out],
        scratch_shapes=[pltpu.VMEM((512, 128), f32)],
        compiler_params=pltpu.CompilerParams(vmem_limit_bytes=40 * 2**20),
        cost_estimate=pl.CostEstimate(
            flops=20 * 10**9, bytes_accessed=4 * 2**20, transcendentals=7 * 10**6
        ),
        name="attend",
    )(info, queries, kv)


def attend_back_kernel(
    info_ref, q_ref, kv_ref, mixed_ref, inverse_ref, grad_ref, dq_ref, dkv_ref, sum_ref, dq_acc
):
    x_block = pl.program_id(0)
    start, cut, low, middle, high = spans(info_ref, x_block)

    @pl.when(x_block == 0)
    def _():
        sum_ref[...] = jnp.zeros_like(sum_ref)

    queries = head_rows(q_ref[:, 0].reshape(256, 128).astype(f32), False).astype(bf16)
    grad = grad_ref[:, 0].reshape(256, 128) * inverse_ref[:, 0].reshape(256, 128)
    grad_rows = head_rows(grad, True)
    product = head_rows(grad * mixed_ref[:, 0].reshape(256, 128), True)
    delta = -jnp.sum(product, axis=1, keepdims=True)
    delta_high = delta.astype(bf16).astype(f32)
    lane = lanes(grad_rows.shape)
    extended = jnp.where(
        lane == 0, delta_high, jnp.where(lane == 1, delta - delta_high, grad_rows)
    ).astype(bf16)
    grad_rows = grad_rows.astype(bf16)
    dq_acc[...] = jnp.zeros_like(dq_acc)

    def step(masked):
        def body(j, carry):
            kv = key_block(kv_ref, j).reshape(KB, 128)
            weights = jnp.exp(dot_nt(kv, queries))
            if masked:
                allowed = allowed_pairs(start, cut, j, 1, weights.shape)
                weights = jnp.where(allowed, weights, 0.0)
            slopes = (weights * dot_nt(with_ones(kv), extended)).astype(bf16)
            total = dot_nn(weights.astype(bf16), grad_rows) + dot_nn(slopes, queries)
            here = (pl.ds(2 * (j % 4), 2), slice(None), j // 4)
            sum_ref[here] = sum_ref[here] + total.reshape(2, 2, 128, 128)
            dq_acc[...] += dot_tn(slopes, kv)
            return carry

        return body

    lax.fori_loop(low, middle, step(True), 0)
    lax.fori_loop(middle, high, step(False), 0)
    step(True)(high, 0)
    sums = dq_acc[...]
    first, second_turned = sums[:256], swing(sums)[256:]
    packed = jnp.where(lanes((256, 128)) < 64, first, second_turned) * DH ** (-0.5)
    dq_ref[...] = packed.reshape(dq_ref.shape)

    @pl.when(x_block == 3)
    def _():
        dkv_ref[...] = sum_ref[...].astype(bf16)


def attend_back(info, queries, kv, mixed, inverse, grad):
    every = (8, 2, 4, 128, 128)
    return pl.pallas_call(
        attend_back_kernel,
        grid=(4,),
        in_specs=[
            pl.BlockSpec(memory_space=pltpu.SMEM),
            chunk_spec(),
            whole_spec(every),
            chunk_spec(),
            chunk_spec(),
            chunk_spec(),
        ],
        out_specs=[chunk_spec(), whole_spec(every)],
        out_shape=[
            jax.ShapeDtypeStruct((2, 4, 128, 128), f32),
            jax.ShapeDtypeStruct(every, bf16),
        ],
        scratch_shapes=[pltpu.VMEM(every, f32), pltpu.VMEM((512, 128), f32)],
        compiler_params=pltpu.CompilerParams(vmem_limit_bytes=48 * 2**20),
        cost_estimate=pl.CostEstimate(
            flops=40 * 10**9, bytes_accessed=8 * 2**20, transcendentals=7 * 10**6
        ),
        name="attend_back",
    )(info, queries, kv, mixed, inverse, grad)


def exchange(blocks, axes):
    return lax.all_to_all(blocks, axes, split_axis=0, concat_axis=0, tiled=True)


def gather(shard, axes):
    count = lax.axis_size(axes)
    return exchange(jnp.broadcast_to(shard[None], (count,) + shard.shape), axes)


def scatter_sum(blocks, axes):
    return jnp.sum(exchange(blocks.astype(bf16), axes).astype(f32), axis=0)


def trade(values):
    return lax.ppermute(values, ("c", "zl"), [(0, 0), (1, 2), (2, 1), (3, 3)])


def rotary_tables(positions):
    halfway = DH // 2
    frequency = theta ** (-(jnp.arange(halfway, dtype=f32) * 2.0 / DH))
    angles = positions.astype(f32)[:, None] * frequency[None, :]
    return jnp.cos(angles)[:, None, :], jnp.sin(angles)[:, None, :]


def head_rope(raw, gains, cosine, sine):
    inverse = lax.rsqrt(jnp.mean(raw * raw, axis=-1, keepdims=True) + epsilon)
    shaped = raw * inverse * gains
    leading, trailing = shaped[..., : DH // 2], shaped[..., DH // 2 :]
    return jnp.concatenate(
        [leading * cosine - trailing * sine, trailing * cosine + leading * sine], axis=-1
    )


def norm_back(unit, inverse, gains, grad):
    scaled = grad * gains
    return inverse * (scaled - unit * jnp.mean(unit * scaled, axis=-1, keepdims=True))


def shards(
    block_input,
    out_grad,
    doc_ids,
    w_query,
    w_key,
    w_value,
    w_out,
    w_gate,
    w_up,
    w_down,
    norm_gains,
    head_gains,
):
    zh, y, c, zl, x = (lax.axis_index(name) for name in AXES)
    block = zh * 4 + y
    member = c * 4 + x

    gains = gather(jnp.concatenate([norm_gains, head_gains]), AXES).astype(f32)
    gain_first = gains[:64, :16].reshape(D)
    gain_second = gains[64:, :16].reshape(D)
    head_gain = gains[:, 16].reshape(2, DH)
    wqkv = trade(jnp.concatenate([w_query, w_key, w_value], axis=1))
    wqkv = gather(wqkv, SHARDS).reshape(D, 256)
    inputs = gather(block_input, GROUP).reshape(1024, D)

    wout_part = gather(trade(w_out), SHARDS).reshape(D, 128)
    wout = jnp.transpose(gather(wout_part, GROUP), (1, 0, 2)).reshape(D, D)
    wgate = lax.all_gather(trade(w_gate), SHARDS, axis=0, tiled=True)
    wup = lax.all_gather(trade(w_up), SHARDS, axis=0, tiled=True)
    wdown = lax.all_gather(trade(w_down.T), SHARDS, axis=0, tiled=True)
    out_grads = gather(out_grad, GROUP).reshape(1024, D)

    offsets = jnp.arange(128, dtype=jnp.int32)
    member_x = jnp.arange(4, dtype=jnp.int32)
    member_c = jnp.arange(2, dtype=jnp.int32)
    positions = (
        member_x[None, :, None] * 2048
        + block * 256
        + member_c[:, None, None] * 128
        + offsets[None, None, :]
    ).reshape(1024)
    cosine, sine = rotary_tables(positions)
    inputs = inputs.astype(f32)
    inverse_first = lax.rsqrt(jnp.mean(inputs * inputs, axis=-1, keepdims=True) + epsilon)
    unit_first = inputs * inverse_first
    normed = (unit_first * gain_first).astype(bf16)
    qkv = dot_nn(normed, wqkv)
    qk_raw = qkv[:, :192].reshape(1024, 3, DH)
    qk_gains = head_gain[jnp.array([0, 0, 1])]

    def turn(raw, gains_now):
        return head_rope(raw, gains_now, cosine, sine)

    qk = turn(qk_raw, qk_gains).astype(bf16)
    queries = (qk[:, :2].reshape(1024, 128) * DH ** (-0.5)).astype(bf16).reshape(2, 4, 128, 128)
    kv_own = jnp.concatenate([qk[:, 2], qkv[:, 192:].astype(bf16)], axis=1)
    kv = gather(kv_own, BLOCKS).reshape(8, 2, 4, 128, 128)
    tokens = jnp.arange(doc_ids.shape[0], dtype=jnp.int32)
    cut = jnp.sum(((tokens // 8192 == zl) & (doc_ids == 2 * zl)).astype(jnp.int32))
    info = jnp.stack([block, cut]).astype(jnp.int32)
    mixed_f32, mixed_own, inverse_sum = attend(info, queries, kv)

    mixed = gather(mixed_own.reshape(1024, 128), GROUP)
    mixed = jnp.transpose(mixed, (1, 0, 2)).reshape(1024, D)
    residual = inputs + dot_nn(mixed, wout)
    inverse_second = lax.rsqrt(jnp.mean(residual * residual, axis=-1, keepdims=True) + epsilon)
    unit_second = residual * inverse_second
    normed_second = (unit_second * gain_second).astype(bf16)
    gate = dot_nn(normed_second, wgate)
    up = dot_nn(normed_second, wup)
    grad_hidden = dot_nn(out_grads, wdown)
    sig = 1.0 / (1.0 + jnp.exp(-gate))
    silu = gate * sig
    hidden = (silu * up).astype(bf16)
    grad_gate = (grad_hidden * up * sig * (1.0 + gate * (1.0 - sig))).astype(bf16)
    grad_up = (grad_hidden * silu).astype(bf16)
    grad_second = dot_nt(grad_gate, wgate) + dot_nt(grad_up, wup)
    gain_second_grad = jnp.sum(grad_second * unit_second, axis=0)
    part = norm_back(unit_second, inverse_second, gain_second, grad_second).reshape(8, 128, D)
    is_own = (jnp.arange(8, dtype=jnp.int32) == member)[:, None, None]
    part = part + jnp.where(is_own, out_grads.astype(f32).reshape(8, 128, D), 0.0)
    part = part.astype(bf16)
    grad_mixed = dot_nt(part.reshape(1024, D), wout).astype(bf16)
    grad_mixed = jnp.transpose(grad_mixed.reshape(1024, 8, 128), (1, 0, 2))
    grad_mixed = scatter_sum(grad_mixed, GROUP).reshape(2, 4, 128, 128)

    grad_q, grad_kv = attend_back(info, queries, kv, mixed_f32, inverse_sum, grad_mixed)

    ffn = dot_nt(hidden, wdown).astype(bf16).reshape(8, 128, D)
    part, ffn, held = lax.optimization_barrier((part, ffn, grad_mixed[0, 0, :8]))
    grad_residual = scatter_sum(part, GROUP)
    ffn = scatter_sum(ffn, GROUP)
    residual_own = lax.dynamic_index_in_dim(
        residual.reshape(8, 128, D), member, 0, keepdims=False
    )
    block_output_value = (residual_own + ffn).astype(bf16)
    grad_attended = grad_residual.astype(bf16).reshape(128, 8, 128)
    grad_attended = exchange(jnp.transpose(grad_attended, (1, 0, 2)), GROUP).reshape(1024, 128)
    grad_wout = dot_tn(mixed, grad_attended)
    grad_wgate = dot_tn(normed_second, grad_gate)
    grad_wup = dot_tn(normed_second, grad_up)
    grad_wdown = dot_tn(out_grads, hidden)

    def settle(grad):
        return trade(scatter_sum(grad.reshape((16, 64) + grad.shape[1:]), SHARDS))

    grad_wgate = settle(grad_wgate)
    grad_wup = settle(grad_wup)
    grad_wdown = settle(grad_wdown).T
    grad_wout = settle(grad_wout)

    grad_kv = scatter_sum(grad_kv.reshape(8, 1024, 128), BLOCKS)
    turned = jnp.concatenate([grad_q.reshape(1024, 128), grad_kv[:, :DH]], axis=1)
    raw_grad, head_grads = jax.vjp(turn, qk_raw, qk_gains)[1](turned.reshape(1024, 3, DH))
    head_grads = jnp.concatenate([head_grads[0] + head_grads[1], head_grads[2]])
    raw_grad = jnp.concatenate(
        [raw_grad.reshape(1024, 192).astype(bf16), grad_kv[:, DH:].astype(bf16)], axis=1
    )
    grad_normed = dot_nt(raw_grad, wqkv)
    gain_first_grad = jnp.sum(grad_normed * unit_first, axis=0)
    grad_normed = scatter_sum(grad_normed.astype(bf16).reshape(8, 128, D), GROUP)
    grad_wqkv = settle(dot_tn(normed, raw_grad))
    own_input = block_input.astype(f32)
    own_inverse = lax.rsqrt(jnp.mean(own_input * own_input, axis=-1, keepdims=True) + epsilon)
    input_grad = grad_residual + norm_back(
        own_input * own_inverse, own_inverse, gain_first, grad_normed
    )
    gain_grads = jnp.concatenate(
        [
            jnp.concatenate([gain_first_grad, gain_second_grad]).reshape(128, 16),
            head_grads.reshape(128, 1),
        ],
        axis=1,
    )
    gain_grads = jnp.sum(exchange(gain_grads, AXES), axis=0)
    return (
        block_output_value,
        input_grad,
        grad_wqkv[:, :128],
        grad_wqkv[:, 128:192],
        grad_wqkv[:, 192:],
        grad_wout,
        grad_wgate,
        grad_wup,
        grad_wdown,
        gain_grads[:16],
        gain_grads[16:],
    )


def solution(mesh):
    fine = Mesh(mesh.devices.reshape(2, 4, 2, 2, 4), AXES)
    rows = P(("zl", "x", "zh", "y", "c"), None)
    weight = P(("zh", "y", "c"), ("zl", "x"))
    down = P(("zl", "x"), ("zh", "y", "c"))
    return jax.shard_map(
        shards,
        mesh=fine,
        in_specs=(rows, rows, P()) + (weight,) * 6 + (down, P(AXES), P(AXES)),
        out_specs=(rows, rows) + (weight,) * 6 + (down, P(AXES), P(AXES)),
        check_vma=False,
    )
```

time: 2450 us -> 666 us (0.27)
  waiting for transfers between devices: 1450 us -> 346 us
  blocking collectives: 270 us -> 34 us
  matrix products: 270 us -> 60.6 us
  local copies, waits for them, and re-layouts: 201 us -> 43 us
  loops' own time: 125 us -> 0 us
  starting transfers between devices: 14.4 us -> 96.7 us
  other arithmetic: 77.8 us -> 24.5 us
  Pallas kernels: 0 us -> 33.9 us
    reduce_scatter x10 -> x0, waiting for transfers between devices: 1010 us -> none  [the longest x1 192 us: shards(): lax.psum_scatter(grad_wgate, 'hd', scatter_dimension=1, tiled=True)]
    all_to_all x3 -> x18, waiting for transfers between devices: 16.7 us -> 255 us  [exchange(): return lax.all_to_all(blocks, axes, split_axis=0, concat_axis=0, tiled=True)]
    unnamed x31 -> x3, waiting for transfers between devices: 236 us -> 0.05 us
    dot_general x245 -> x15, matrix products: 270 us -> 60.6 us  [contract(): lax.dot_general(left, right, ((dims[0], dims[1]), ((), ())), preferred_el...]
    all_gather x5 -> x0, blocking collectives: 133 us -> none  [the longest x1 29.1 us: shards(): lax.all_gather(w_value, 'hd', axis=1, tiled=True)]
    another operation x3 -> x0, loops' own time: 125 us -> none  [the longest x1 43 us: shards(): stat_pair, ignored = lax.scan(stats_step, (stat_start, stat_start), sources)]
    dynamic_slice x145 -> x0, local copies, waits for them, and re-layouts: 118 us -> none  [the longest x48 46.7 us: key_parts(): lax.dynamic_slice_in_dim(kv_every, source * head_rows, head_rows, 0)]
    unnamed x4 -> x0, blocking collectives: 106 us -> none
  transfers between devices with their start and end apart: 29 -> 31, of which waited for: 21 -> 18; matrix products, arithmetic and copies ran while one was open for 12% -> 15% of each run, Pallas kernels for 0% -> 5%
where the time goes in v1:
time: 666 us; the launch traced here: 655 us
  waiting for transfers between devices  346 us (52%)
  starting transfers between devices  96.7 us (15%)
  matrix products  60.6 us (9%)
  local copies, waits for them, and re-layouts  43 us (6%)
  blocking collectives  34 us (5%)
  Pallas kernels  33.9 us (5%)
  other arithmetic  24.5 us (4%)
  between operations  15.9 us (2%)
    all_to_all x18, waiting for transfers between devices, exchange(): return lax.all_to_all(blocks, axes, split_axis=0, concat_axis=0, tiled=True)  255 us
    all_to_all x18, starting transfers between devices, exchange(): return lax.all_to_all(blocks, axes, split_axis=0, concat_axis=0, tiled=True)  89 us
    all_gather x1, waiting for transfers between devices, shards(): wup = lax.all_gather(trade(w_up), SHARDS, axis=0, tiled=True)  73.4 us
    dot_general x15, matrix products, contract(): lax.dot_general(left, right, ((dims[0], dims[1]), ((), ())), preferred_el...  60.6 us
    all_to_all x2, blocking collectives, exchange(): return lax.all_to_all(blocks, axes, split_axis=0, concat_axis=0, tiled=True)  34 us
    pallas_call x1, Pallas kernels, attend_back(): pl.pallas_call(attend_back_kernel, grid=(4,), in_specs=[pl.BlockSpec(memo...  22.7 us
    all_gather x1, waiting for transfers between devices, shards(): wgate = lax.all_gather(trade(w_gate), SHARDS, axis=0, tiled=True)  17.9 us
    unnamed x102, local copies, waits for them, and re-layouts  13.8 us
  transfers between devices with their start and end apart: 31, of which 18 were waited for; matrix products, arithmetic and copies ran while one was open for 15% of the time, Pallas kernels for 5%

profile of v1, /device:TPU:0, one launch (start us, length us, event | category | flops | bytes accessed | tf_op | source)
XLA Modules:
  0.0 654.5 jit_solution(6859377730424055774)
XLA Ops:
  10.0 21.9 %all_to_all.105 = bf16[128,1,17]{2,1,0:T(2,128)(2,1)S(1)} all-to-all(bf16[128,1,17]{2,1,0:T(2,128)(2,1)S(1)} %broadcast_in_dim.33), channel_id=1, replica_groups=mesh['zh'=2,'y'=4,'c'=2,'zl'=2,'x'=4] {'zh','y','c','zl','x'}, dimensions={0} | all-to-all | bytes 8704 | tf_op jit(solution)/shard_map/all_to_all | solution.py:233
  32.0 12.1 %all_to_all.106 = bf16[16,64,128]{2,1,0:T(8,128)(2,1)} all-to-all(bf16[16,64,128]{2,1,0:T(8,128)(2,1)S(1)} %broadcast_in_dim.39), channel_id=1, replica_groups=mesh['zh'=2,'y'=4,'c'=2,'zl'=2,'x'=4] {'zh','y','zl'}, dimensions={0} | all-to-all | bytes 524288 | tf_op jit(solution)/shard_map/all_to_all | solution.py:233
  52.7 24.2 %all-to-all-done = bf16[8,128,1024]{2,1,0:T(8,128)(2,1)S(1)} async-done(((bf16[8,128,1024]{2,1,0:T(8,128)(2,1)}), bf16[8,128,1024]{2,1,0:T(8,128)(2,1)S(1)}, u32[]{:S(2)}, u32[]{:S(2)}) %all-to-all-start) | async-done | bytes 2097184 | tf_op jit(solution)/shard_map/all_to_all | solution.py:233
  84.1 9.3 %all-to-all-done.2 = bf16[16,64,256]{2,1,0:T(8,128)(2,1)S(1)} async-done(((bf16[16,64,256]{2,1,0:T(8,128)(2,1)}), bf16[16,64,256]{2,1,0:T(8,128)(2,1)S(1)}, u32[]{:S(2)}, u32[]{:S(2)}) %all-to-all-start.2) | async-done | bytes 524320 | tf_op jit(solution)/shard_map/all_to_all | solution.py:233
  103.0 22.9 %all-to-all-done.7 = bf16[8,128,1024]{2,1,0:T(8,128)(2,1)} async-done(((bf16[8,128,1024]{2,1,0:T(8,128)(2,1)}), bf16[8,128,1024]{2,1,0:T(8,128)(2,1)}, u32[]{:S(2)}, u32[]{:S(2)}) %all-to-all-start.7) | async-done | bytes 2097184 | tf_op jit(solution)/shard_map/all_to_all | solution.py:233
  134.7 28.9 %all-to-all-done.3 = bf16[8,1024,128]{2,1,0:T(8,128)(2,1)S(1)} async-done(((bf16[8,1024,128]{2,1,0:T(8,128)(2,1)}), bf16[8,1024,128]{2,1,0:T(8,128)(2,1)S(1)}, u32[]{:S(2)}, u32[]{:S(2)}) %all-to-all-start.3) | async-done | bytes 2097184 | tf_op jit(solution)/shard_map/all_to_all | solution.py:233
  169.8 11.2 %attend.1 = (f32[2,4,128,128]{3,2,1,0:T(8,128)S(1)}, bf16[2,4,128,128]{3,2,1,0:T(8,128)(2,1)S(1)}, f32[2,4,128,128]{3,2,1,0:T(8,128)S(1)}) custom-call(s32[2]{0:T(128)S(1)} %pad_add_fusion.1.info_ref, bf16[2,4,128,128]{3,2,1,0:T(8,128)(2,1)S(1)} %copy.59.q_ref, bf16[8,2,4,128,128]{4,3,2,1,0:T(8,128)(2,1)S(1)} %bitcast.118), custom_call_target="tpu_custom_call" | custom-call | flops 20000000000 | bytes 4194304 | tf_op jit(solution)/shard_map/attend/pallas_call | solution.py:134
  182.1 14.4 %all-to-all-done.6 = bf16[8,1024,128]{1,2,0:T(8,128)(2,1)} async-done(((bf16[8,1024,128]{1,2,0:T(8,128)(2,1)}), bf16[8,1024,128]{1,2,0:T(8,128)(2,1)}, u32[]{:S(2)}, u32[]{:S(2)}) %all-to-all-start.6) | async-done | bytes 2097184 | tf_op jit(solution)/shard_map/all_to_all | solution.py:233
  198.0 4.5 all-to-all-start.4
  204.2 5.0 fusion.35
  209.2 19.9 %all-to-all-done.4 = bf16[8,1024,128]{1,2,0:T(8,128)(2,1)} async-done(((bf16[8,1024,128]{1,2,0:T(8,128)(2,1)}), bf16[8,1024,128]{1,2,0:T(8,128)(2,1)}, u32[]{:S(2)}, u32[]{:S(2)}) %all-to-all-start.4) | async-done | bytes 2097184 | tf_op jit(solution)/shard_map/all_to_all | solution.py:233
  229.1 4.8 multiply_reduce_fusion.2
  236.3 17.9 %all-gather.8.cloned.1.call-done = bf16[1024,576]{1,0:T(8,128)(2,1)} async-done(((bf16[64,576]{1,0:T(8,128)(2,1)}), bf16[1024,576]{1,0:T(8,128)(2,1)}) %all-gather.8.cloned.1.call-update) | async-done | bytes 1179664 | tf_op jit(solution)/shard_map/all_gather | solution.py:298
  258.5 73.4 %all-gather.6.cloned.1.call-done = bf16[1024,576]{1,0:T(8,128)(2,1)} async-done(((bf16[64,576]{1,0:T(8,128)(2,1)}), bf16[1024,576]{1,0:T(8,128)(2,1)}) %all-gather.6.cloned.1.call-update) | async-done | bytes 1179664 | tf_op jit(solution)/shard_map/all_gather | solution.py:299
  331.9 6.6 %multiply_convert_fusion.1 = (bf16[1024,576]{0,1:T(8,128)(2,1)S(1)}, bf16[1024,576]{0,1:T(8,128)(2,1)}, bf16[1024,576]{0,1:T(8,128)(2,1)}) fusion(f32[1024,576]{0,1:T(8,128)} %fusion.36, f32[1024,576]{0,1:T(8,128)} %fusion.35, bf16[1024,1024]{1,0:T(8,128)(2,1)S(1)} %multiply_convert_fusion, bf16[1024,576]{1,0:T(8,128)(2,1)} %all-gather.6.cloned.1.call-done), kind=kOutput, calls=%fused_computation.26 | convolution fusion | flops 1216806912 | bytes 11534336 | tf_op jit(solution)/shard_map/dot_general | solution.py:29
  343.9 6.5 all-to-all-start.18
  361.6 5.3 convolution_convert_fusion
  379.1 19.7 %all-to-all-done.10 = bf16[8,1024,128]{1,2,0:T(8,128)(2,1)S(1)} async-done(((bf16[8,1024,128]{1,2,0:T(8,128)(2,1)}), bf16[8,1024,128]{1,2,0:T(8,128)(2,1)S(1)}, u32[]{:S(2)}, u32[]{:S(2)}) %all-to-all-start.10) | async-done | bytes 2097184 | tf_op jit(solution)/shard_map/all_to_all | solution.py:233
  398.8 7.4 %all-to-all-start.17 = ((bf16[16,64,576]{2,1,0:T(8,128)(2,1)}), bf16[16,64,576]{2,1,0:T(8,128)(2,1)}, u32[]{:S(2)}, u32[]{:S(2)}) async-start(bf16[16,64,576]{2,1,0:T(8,128)(2,1)} %bitcast.132), calls=%async_computation.17 | async-start | bytes 2621440 | tf_op jit(solution)/shard_map/all_to_all | solution.py:233
  413.6 14.5 %all-to-all-done.17 = bf16[16,64,576]{2,1,0:T(8,128)(2,1)} async-done(((bf16[16,64,576]{2,1,0:T(8,128)(2,1)}), bf16[16,64,576]{2,1,0:T(8,128)(2,1)}, u32[]{:S(2)}, u32[]{:S(2)}) %all-to-all-start.17) | async-done | bytes 1179680 | tf_op jit(solution)/shard_map/all_to_all | solution.py:233
  428.1 4.7 all-to-all-start.16
  432.8 22.7 %attend_back.1 = (f32[2,4,128,128]{3,2,1,0:T(8,128)S(1)}, bf16[8,2,4,128,128]{4,3,2,1,0:T(8,128)(2,1)}) custom-call(s32[2]{0:T(128)S(1)} %pad_add_fusion.1.info_ref, bf16[2,4,128,128]{3,2,1,0:T(8,128)(2,1)S(1)} %copy.59.q_ref, bf16[8,2,4,128,128]{4,3,2,1,0:T(8,128)(2,1)} %bitcast.119, f32[2,4,128,128]{3,2,1,0:T(8,128)S(1)} %get-tuple-element.21.mixed_ref, ...), custom_call_target="tpu_custom_call" | custom-call | flops 40000000000 | bytes 8388608 | tf_op jit(solution)/shard_map/attend_back/pallas_call | solution.py:207
  455.5 10.3 %all-to-all-start.11 = ((bf16[8,1024,128]{2,1,0:T(8,128)(2,1)}), bf16[8,1024,128]{2,1,0:T(8,128)(2,1)S(1)}, u32[]{:S(2)}, u32[]{:S(2)}) async-start(bf16[8,1024,128]{2,1,0:T(8,128)(2,1)} %bitcast.28), calls=%async_computation.11 | async-start | bytes 4194304 | tf_op jit(solution)/shard_map/all_to_all | solution.py:233
  465.7 4.9 convolution_convert_fusion.1
  470.7 22.8 %all-to-all-done.11 = bf16[8,1024,128]{2,1,0:T(8,128)(2,1)S(1)} async-done(((bf16[8,1024,128]{2,1,0:T(8,128)(2,1)}), bf16[8,1024,128]{2,1,0:T(8,128)(2,1)S(1)}, u32[]{:S(2)}, u32[]{:S(2)}) %all-to-all-start.11) | async-done | bytes 2097184 | tf_op jit(solution)/shard_map/all_to_all | solution.py:233
  508.0 16.4 %all-to-all-done.9 = bf16[8,128,1024]{2,1,0:T(8,128)(2,1)} async-done(((bf16[8,128,1024]{2,1,0:T(8,128)(2,1)}), bf16[8,128,1024]{2,1,0:T(8,128)(2,1)}, u32[]{:S(2)}, u32[]{:S(2)}) %all-to-all-start.9) | async-done | bytes 2097184 | tf_op jit(solution)/shard_map/all_to_all | solution.py:233
  532.7 22.0 %all-to-all-done.12 = bf16[8,128,1024]{2,1,0:T(8,128)(2,1)S(1)} async-done(((bf16[8,128,1024]{2,1,0:T(8,128)(2,1)}), bf16[8,128,1024]{2,1,0:T(8,128)(2,1)S(1)}, u32[]{:S(2)}, u32[]{:S(2)}) %all-to-all-start.12) | async-done | bytes 2097184 | tf_op jit(solution)/shard_map/all_to_all | solution.py:233
  571.4 14.7 %all-to-all-done.8 = bf16[8,128,1024]{2,1,0:T(8,128)(2,1)S(1)} async-done(((bf16[8,128,1024]{2,1,0:T(8,128)(2,1)}), bf16[8,128,1024]{2,1,0:T(8,128)(2,1)S(1)}, u32[]{:S(2)}, u32[]{:S(2)}) %all-to-all-start.8) | async-done | bytes 2097184 | tf_op jit(solution)/shard_map/all_to_all | solution.py:233
  586.1 9.3 %all-to-all-start.19 = ((f32[128,1,17]{2,1,0:T(1,128)}), f32[128,1,17]{2,1,0:T(1,128)S(1)}, u32[]{:S(2)}, u32[]{:S(2)}) async-start(f32[128,1,17]{2,1,0:T(1,128)} %bitcast.52), calls=%async_computation.19 | async-start | bytes 131072 | tf_op jit(solution)/shard_map/all_to_all | solution.py:233
  597.2 7.4 %all-to-all-done.19 = f32[128,1,17]{2,1,0:T(1,128)S(1)} async-done(((f32[128,1,17]{2,1,0:T(1,128)}), f32[128,1,17]{2,1,0:T(1,128)S(1)}, u32[]{:S(2)}, u32[]{:S(2)}) %all-to-all-start.19) | async-done | bytes 8736 | tf_op jit(solution)/shard_map/all_to_all | solution.py:233
  622.1 8.7 %all-to-all-done.13 = bf16[16,64,256]{2,1,0:T(8,128)(2,1)S(1)} async-done(((bf16[16,64,256]{2,1,0:T(8,128)(2,1)}), bf16[16,64,256]{2,1,0:T(8,128)(2,1)S(1)}, u32[]{:S(2)}, u32[]{:S(2)}) %all-to-all-start.13) | async-done | bytes 524320 | tf_op jit(solution)/shard_map/all_to_all | solution.py:233
  637.7 5.2 all-to-all-done.15
  (246 shorter events, 159.2 us)
Async XLA Ops:
  7.2 24.7 %collective-permute-start.1 = (bf16[64,128]{1,0:T(8,128)(2,1)}, bf16[64,128]{1,0:T(8,128)(2,1)S(1)}, u32[]{:S(2)}, u32[]{:S(2)}) collective-permute-start(bf16[64,128]{1,0:T(8,128)(2,1)} %param.19), channel_id=1, source_target_pairs={{0,0},{4,8},{8,4},{12,12},{1,1},{5,9},{9,5},{13,13},{2,2},{6,10},{... | collective-permute-start | bytes 49160 | tf_op jit(solution)/shard_map/ppermute | solution.py:246
  46.6 30.3 %all-to-all-start = ((bf16[8,128,1024]{2,1,0:T(8,128)(2,1)}), bf16[8,128,1024]{2,1,0:T(8,128)(2,1)S(1)}, u32[]{:S(2)}, u32[]{:S(2)}) async-start(bf16[8,128,1024]{2,1,0:T(8,128)(2,1)} %broadcast_in_dim.32), calls=%async_computation | async-start | bytes 4194304 | tf_op jit(solution)/shard_map/all_to_all | solution.py:233
  50.5 2.2 collective-permute-start
  51.1 31.8 %collective-permute-start.2 = (bf16[64,576]{1,0:T(8,128)(2,1)S(1)}, bf16[64,576]{1,0:T(8,128)(2,1)S(1)}, u32[]{:S(2)}, u32[]{:S(2)}) collective-permute-start(bf16[64,576]{1,0:T(8,128)(2,1)S(1)} %bitcast.151), channel_id=1, source_target_pairs={{0,0},{4,8},{8,4},{12,12},{1,1},{5,9},{9,5},{13,13},{2,2},{6,10},{... | collective-permute-start | bytes 221192 | tf_op jit(solution)/shard_map/ppermute | solution.py:246
  77.8 15.7 %all-to-all-start.2 = ((bf16[16,64,256]{2,1,0:T(8,128)(2,1)}), bf16[16,64,256]{2,1,0:T(8,128)(2,1)S(1)}, u32[]{:S(2)}, u32[]{:S(2)}) async-start(bf16[16,64,256]{2,1,0:T(8,128)(2,1)} %broadcast_in_dim.34), calls=%async_computation.2 | async-start | bytes 1048576 | tf_op jit(solution)/shard_map/all_to_all | solution.py:233
  81.3 122.8 %all-gather.4.cloned.1.call-start = ((), (), s32[]{:S(2)}) async-start(), calls=%async_computation.20 | async-start | bytes 1392640 | tf_op jit(solution)/shard_map/all_gather | solution.py:300
  95.0 30.9 %all-to-all-start.7 = ((bf16[8,128,1024]{2,1,0:T(8,128)(2,1)}), bf16[8,128,1024]{2,1,0:T(8,128)(2,1)}, u32[]{:S(2)}, u32[]{:S(2)}) async-start(bf16[8,128,1024]{2,1,0:T(8,128)(2,1)} %broadcast_in_dim.42), calls=%async_computation.7 | async-start | bytes 4194304 | tf_op jit(solution)/shard_map/all_to_all | solution.py:233
  127.5 36.1 %all-to-all-start.3 = ((bf16[8,1024,128]{2,1,0:T(8,128)(2,1)}), bf16[8,1024,128]{2,1,0:T(8,128)(2,1)S(1)}, u32[]{:S(2)}, u32[]{:S(2)}) async-start(bf16[8,1024,128]{2,1,0:T(8,128)(2,1)} %broadcast_in_dim.36), calls=%async_computation.3 | async-start | bytes 4194304 | tf_op jit(solution)/shard_map/all_to_all | solution.py:233
  131.3 123.0 %all-gather.8.cloned.1.call-start = ((), (), s32[]{:S(2)}) async-start(), calls=%async_computation.22 | async-start | bytes 1392640 | tf_op jit(solution)/shard_map/all_gather | solution.py:298
  131.3 2.1 collective-permute-start.4
  165.5 30.9 %all-to-all-start.6 = ((bf16[8,1024,128]{1,2,0:T(8,128)(2,1)}), bf16[8,1024,128]{1,2,0:T(8,128)(2,1)}, u32[]{:S(2)}, u32[]{:S(2)}) async-start(bf16[8,1024,128]{1,2,0:T(8,128)(2,1)} %broadcast_in_dim.41), calls=%async_computation.6 | async-start | bytes 4194304 | tf_op jit(solution)/shard_map/all_to_all | solution.py:233
  198.0 31.1 %all-to-all-start.4 = ((bf16[8,1024,128]{1,2,0:T(8,128)(2,1)}), bf16[8,1024,128]{1,2,0:T(8,128)(2,1)}, u32[]{:S(2)}, u32[]{:S(2)}) async-start(bf16[8,1024,128]{1,2,0:T(8,128)(2,1)} %broadcast_in_dim.38), calls=%async_computation.4 | async-start | bytes 4194304 | tf_op jit(solution)/shard_map/all_to_all | solution.py:233
  202.5 129.4 %all-gather.6.cloned.1.call-start = ((), (), s32[]{:S(2)}) async-start(), calls=%async_computation.21 | async-start | bytes 1392640 | tf_op jit(solution)/shard_map/all_gather | solution.py:299
  202.6 0.8 collective-permute-start.3
  236.3 95.6 %copy-start.16 = (bf16[1024,1024]{1,0:T(8,128)(2,1)}, bf16[1024,1024]{1,0:T(8,128)(2,1)S(1)}, u32[]{:S(2)}) copy-start(bf16[1024,1024]{1,0:T(8,128)(2,1)S(1)} %multiply_convert_fusion) | copy-start | bytes 6291460
  343.9 23.0 %all-to-all-start.18 = ((bf16[16,64,576]{2,1,0:T(8,128)(2,1)}), bf16[16,64,576]{2,1,0:T(8,128)(2,1)S(1)}, u32[]{:S(2)}, u32[]{:S(2)}) async-start(bf16[16,64,576]{2,1,0:T(8,128)(2,1)} %bitcast.45), calls=%async_computation.18 | async-start | bytes 2621440 | tf_op jit(solution)/shard_map/all_to_all | solution.py:233
  368.0 30.8 %all-to-all-start.10 = ((bf16[8,1024,128]{1,2,0:T(8,128)(2,1)}), bf16[8,1024,128]{1,2,0:T(8,128)(2,1)S(1)}, u32[]{:S(2)}, u32[]{:S(2)}) async-start(bf16[8,1024,128]{1,2,0:T(8,128)(2,1)} %bitcast.141), calls=%async_computation.10 | async-start | bytes 4194304 | tf_op jit(solution)/shard_map/all_to_all | solution.py:233
  398.8 29.3 %all-to-all-start.17 = ((bf16[16,64,576]{2,1,0:T(8,128)(2,1)}), bf16[16,64,576]{2,1,0:T(8,128)(2,1)}, u32[]{:S(2)}, u32[]{:S(2)}) async-start(bf16[16,64,576]{2,1,0:T(8,128)(2,1)} %bitcast.132), calls=%async_computation.17 | async-start | bytes 2621440 | tf_op jit(solution)/shard_map/all_to_all | solution.py:233
  428.1 27.4 %all-to-all-start.16 = ((bf16[16,64,576]{2,1,0:T(8,128)(2,1)}), bf16[16,64,576]{2,1,0:T(8,128)(2,1)}, u32[]{:S(2)}, u32[]{:S(2)}) async-start(bf16[16,64,576]{2,1,0:T(8,128)(2,1)} %bitcast.131), calls=%async_computation.16 | async-start | bytes 2621440 | tf_op jit(solution)/shard_map/all_to_all | solution.py:233
  455.5 38.0 %all-to-all-start.11 = ((bf16[8,1024,128]{2,1,0:T(8,128)(2,1)}), bf16[8,1024,128]{2,1,0:T(8,128)(2,1)S(1)}, u32[]{:S(2)}, u32[]{:S(2)}) async-start(bf16[8,1024,128]{2,1,0:T(8,128)(2,1)} %bitcast.28), calls=%async_computation.11 | async-start | bytes 4194304 | tf_op jit(solution)/shard_map/all_to_all | solution.py:233
  493.5 30.9 %all-to-all-start.9 = ((bf16[8,128,1024]{2,1,0:T(8,128)(2,1)}), bf16[8,128,1024]{2,1,0:T(8,128)(2,1)}, u32[]{:S(2)}, u32[]{:S(2)}) async-start(bf16[8,128,1024]{2,1,0:T(8,128)(2,1)} %copy-done.11), calls=%async_computation.9 | async-start | bytes 4194304 | tf_op jit(solution)/shard_map/all_to_all | solution.py:233
  524.4 30.2 %all-to-all-start.12 = ((bf16[8,128,1024]{2,1,0:T(8,128)(2,1)}), bf16[8,128,1024]{2,1,0:T(8,128)(2,1)S(1)}, u32[]{:S(2)}, u32[]{:S(2)}) async-start(bf16[8,128,1024]{2,1,0:T(8,128)(2,1)} %bitcast.140), calls=%async_computation.12 | async-start | bytes 4194304 | tf_op jit(solution)/shard_map/all_to_all | solution.py:233
  529.8 32.1 %collective-permute-start.9 = (f32[64,576]{1,0:T(8,128)S(1)}, f32[64,576]{1,0:T(8,128)S(1)}, u32[]{:S(2)}, u32[]{:S(2)}) collective-permute-start(f32[64,576]{1,0:T(8,128)S(1)} %convert_reduce_fusion.5), channel_id=1, source_target_pairs={{0,0},{4,8},{8,4},{12,12},{1,1},{5,9},{9,5},{13,13},{2,2},{6,10},{... | collective-permute-start | bytes 442376 | tf_op jit(solution)/shard_map/ppermute | solution.py:246
  532.0 29.9 %collective-permute-start.7 = (f32[64,576]{1,0:T(8,128)S(1)}, f32[64,576]{1,0:T(8,128)S(1)}, u32[]{:S(2)}, u32[]{:S(2)}) collective-permute-start(f32[64,576]{1,0:T(8,128)S(1)} %convert_reduce_fusion.7), channel_id=1, source_target_pairs={{0,0},{4,8},{8,4},{12,12},{1,1},{5,9},{9,5},{13,13},{2,2},{6,10},{... | collective-permute-start | bytes 442376 | tf_op jit(solution)/shard_map/ppermute | solution.py:246
  556.0 30.1 %all-to-all-start.8 = ((bf16[8,128,1024]{2,1,0:T(8,128)(2,1)}), bf16[8,128,1024]{2,1,0:T(8,128)(2,1)S(1)}, u32[]{:S(2)}, u32[]{:S(2)}) async-start(bf16[8,128,1024]{2,1,0:T(8,128)(2,1)} %bitcast.137), calls=%async_computation.8 | async-start | bytes 4194304 | tf_op jit(solution)/shard_map/all_to_all | solution.py:233
  561.1 0.9 collective-permute-start.8
  586.1 18.5 %all-to-all-start.19 = ((f32[128,1,17]{2,1,0:T(1,128)}), f32[128,1,17]{2,1,0:T(1,128)S(1)}, u32[]{:S(2)}, u32[]{:S(2)}) async-start(f32[128,1,17]{2,1,0:T(1,128)} %bitcast.52), calls=%async_computation.19 | async-start | bytes 131072 | tf_op jit(solution)/shard_map/all_to_all | solution.py:233
  604.6 10.6 %all-to-all-start.14 = ((bf16[8,128,128]{2,1,0:T(8,128)(2,1)}), bf16[8,128,128]{2,1,0:T(8,128)(2,1)S(1)}, u32[]{:S(2)}, u32[]{:S(2)}) async-start(bf16[8,128,128]{2,1,0:T(8,128)(2,1)} %bitcast.115), calls=%async_computation.14 | async-start | bytes 524288 | tf_op jit(solution)/shard_map/all_to_all | solution.py:233
  615.2 15.7 %all-to-all-start.13 = ((bf16[16,64,256]{2,1,0:T(8,128)(2,1)}), bf16[16,64,256]{2,1,0:T(8,128)(2,1)S(1)}, u32[]{:S(2)}, u32[]{:S(2)}) async-start(bf16[16,64,256]{2,1,0:T(8,128)(2,1)} %convolution_convert_fusion.5), calls=%async_computation.13 | async-start | bytes 1048576 | tf_op jit(solution)/shard_map/all_to_all | solution.py:233
  630.8 12.0 %all-to-all-start.15 = ((bf16[16,64,128]{2,1,0:T(8,128)(2,1)}), bf16[16,64,128]{2,1,0:T(8,128)(2,1)S(1)}, u32[]{:S(2)}, u32[]{:S(2)}) async-start(bf16[16,64,128]{2,1,0:T(8,128)(2,1)} %convolution_convert_fusion.6), calls=%async_computation.15 | async-start | bytes 524288 | tf_op jit(solution)/shard_map/all_to_all | solution.py:233
  637.0 6.6 %collective-permute-start.5 = (f32[64,256]{1,0:T(8,128)S(1)}, f32[64,256]{1,0:T(8,128)S(1)}, u32[]{:S(2)}, u32[]{:S(2)}) collective-permute-start(f32[64,256]{1,0:T(8,128)S(1)} %convert_reduce_fusion.8), channel_id=1, source_target_pairs={{0,0},{4,8},{8,4},{12,12},{1,1},{5,9},{9,5},{13,13},{2,2},{6,10},{... | collective-permute-start | bytes 196616 | tf_op jit(solution)/shard_map/ppermute | solution.py:246
  642.9 2.0 collective-permute-start.6
  (48 other events, 359.2 us)
Sparse Core Ops, SparseCore 0:
  84.4 91.5 all-gather.3
  178.2 76.0 all-gather.7
  256.5 75.3 all-gather.5
